TPU v7x, 32 devices: a whole 2x2x4 slice. The times are simulated.
32 devices in a mesh: grp: 2 (over y), exp: 8 (over z, core), lat: 2 (over x).
Axes of the slice: x: 2, y: 2, z: 4, core: 2. Of those that a mesh axis runs over, the one named last changes fastest.
Arguments:
- tokens: bfloat16 [128, 2880], P(('grp', 'exp'), 'lat'), parts along dimension 0, may hold values from -6 to 6
- routes: int32 [128, 4], P(('grp', 'exp')), parts along dimension 0, may hold values from 0 to 7, all different within a row; in each aligned block of 8 rows (0 to 7, 8 to 15, ...) at most 5 rows name the same one
- gates: float32 [128, 4], P(('grp', 'exp')), parts along dimension 0, may hold values from 0.1 to 1
- w_gate: bfloat16 [8, 2880, 1440], P('exp', None, 'lat'), may hold values from -0.109375 to 0.109375
- w_up: bfloat16 [8, 2880, 1440], P('exp', None, 'lat'), may hold values from -0.109375 to 0.109375
- w_down: bfloat16 [8, 1440, 2880], P('exp', 'lat'), may hold values from -0.15625 to 0.15625
- w_enc: bfloat16 [2880, 32768], P('lat', 'exp'), may hold values from -0.109375 to 0.109375
- b_enc: float32 [32768], P('exp'), may hold values from -3 to 3
- w_dec: bfloat16 [32768, 2880], P('exp', 'lat'), may hold values from -0.03125 to 0.03125
- b_dec: float32 [2880], P('lat'), may hold values from -3 to 3
Outputs:
- moe_out: bfloat16 [128, 2880], P(('grp', 'exp'), 'lat'), parts along dimension 0
- codes: bfloat16 [128, 32768], P(('grp', 'lat'), 'exp'), parts along dimension 0
- error: float32 [128, 2880], P(('grp', 'exp'), 'lat'), parts along dimension 0
There are 2 independent parts, one for each index of `grp`. A program takes and returns all parts, laid end to end along the dimension named above; an argument that names none is the same for every part. Nothing has to cross between parts.
Inputs may be any that keep to these rules, and one draw needn't show every extreme that they name: `routes`: each row names 4 different experts and every expert is named by some row. Within each aligned block of 8 rows no expert is named by more than 5 rows; in some block some expert is named by exactly 5 rows.
All inputs are finite; a program needn't handle non-finite values.
Results may differ from a plain program's by a relative error of at most 0.013.
Values may be sent and summed in bfloat16 or wider, within the bound.
A program may use at most 128 MiB of HBM per device.

v0:
```python
import jax
import jax.numpy as jnp
from jax import lax
from jax.sharding import PartitionSpec as P


def expert_hidden(gate_sum, up_sum):
    return (gate_sum * jax.nn.sigmoid(1.702 * gate_sum) * (up_sum + 1.0)).astype(jnp.bfloat16)


def combine_rows(returned, slot_index, gates):
    row_count = gates.shape[0]
    top_count = gates.shape[1]
    picked = jnp.take(returned, slot_index, axis=0).reshape(row_count, top_count, returned.shape[1])
    return jnp.sum(picked * gates[:, :, None], axis=1)


def per_device(tokens, routes, gates, w_gate, w_up, w_down, w_enc, b_enc, w_dec, b_dec):
    row_count = tokens.shape[0]
    top_count = routes.shape[1]
    experts = lax.axis_size("exp")
    slots_per = min(row_count, row_count * top_count // experts + 1)
    total_slots = experts * slots_per
    flat_expert = routes.reshape(-1)
    onehot = (flat_expert[:, None] == jnp.arange(experts, dtype=jnp.int32)[None, :]).astype(
        jnp.int32
    )
    before = jnp.cumsum(onehot, axis=0) - onehot
    rank_in = jnp.sum(before * onehot, axis=1)
    slot_index = flat_expert * slots_per + rank_in
    placing = (jnp.arange(total_slots, dtype=jnp.int32)[:, None] == slot_index[None, :]).astype(
        jnp.bfloat16
    )
    outgoing = jnp.dot(
        placing, jnp.repeat(tokens, top_count, axis=0), preferred_element_type=jnp.float32
    ).astype(jnp.bfloat16)
    arrived = lax.all_to_all(outgoing, "exp", split_axis=0, concat_axis=0, tiled=True)
    block_in = lax.all_gather(arrived, "lat", axis=1, tiled=True)
    gate_rows = w_gate[0]
    up_rows = w_up[0]
    gate_sum = jnp.dot(block_in, gate_rows, preferred_element_type=jnp.float32)
    up_sum = jnp.dot(block_in, up_rows, preferred_element_type=jnp.float32)
    hidden = expert_hidden(gate_sum, up_sum)
    partial_value = jnp.dot(hidden, w_down[0], preferred_element_type=jnp.float32)
    gathered = lax.all_gather(tokens, "exp", axis=0, tiled=True)
    block_in = gathered
    pre = lax.psum_scatter(
        jnp.dot(block_in, w_enc, preferred_element_type=jnp.float32),
        "lat",
        scatter_dimension=0,
        tiled=True,
    )
    codes = jnp.maximum(pre + b_enc[None, :], 0.0).astype(jnp.bfloat16)
    shares = lax.psum_scatter(partial_value, "lat", scatter_dimension=1, tiled=True)
    returned = lax.all_to_all(shares, "exp", split_axis=0, concat_axis=0, tiled=True)
    moe_local = combine_rows(returned, slot_index, gates)
    moe_out = moe_local.astype(jnp.bfloat16)
    partial_recon = jnp.dot(
        lax.all_gather(codes, "lat", axis=0, tiled=True), w_dec, preferred_element_type=jnp.float32
    )
    recon = (
        lax.psum_scatter(
            partial_recon.astype(jnp.bfloat16), "exp", scatter_dimension=0, tiled=True
        ).astype(jnp.float32)
        + b_dec[None, :]
    )
    error = moe_out.astype(jnp.float32) - recon
    return (moe_out, codes, error)


def solution(mesh):
    placed = (
        P(("grp", "exp"), "lat"),
        P(("grp", "exp"), None),
        P(("grp", "exp"), None),
        P("exp", None, "lat"),
        P("exp", None, "lat"),
        P("exp", "lat", None),
        P("lat", "exp"),
        P("exp"),
        P("exp", "lat"),
        P("lat"),
    )
    return jax.shard_map(
        per_device,
        mesh=mesh,
        in_specs=placed,
        out_specs=(P(("grp", "exp"), "lat"), P(("grp", "lat"), "exp"), P(("grp", "exp"), "lat")),
        check_vma=False,
    )
```

profile of v0, /device:TPU:0, one launch (start us, length us, event | category | flops | bytes accessed | tf_op | source)
XLA Modules:
  0.0 144.7 jit_solution(203402444249438012)
XLA Ops:
  7.2 0.0 reduce-scatter.10.cloned.1.call-start
  7.2 0.8 copy.20
  8.0 0.1 reshape.70
  8.0 0.1 fusion.28
  8.1 0.1 reduce_window_sum.11
  8.2 0.2 select_reduce_fusion
  8.4 0.8 broadcast_in_dim.20
  9.2 0.2 convolution_convert_fusion.1
  9.3 0.1 all_to_all.16
  9.4 14.5 %all_to_all.24 = bf16[8,5,1440]{2,1,0:T(8,128)(2,1)S(1)} all-to-all(bf16[8,5,1440]{2,1,0:T(8,128)(2,1)S(1)} %all_to_all.16), channel_id=1, replica_groups=mesh['grp'=2,'exp'=8,'lat'=2] {'exp'}, dimensions={0} | all-to-all | bytes 230400 | tf_op jit(solution)/shard_map/all_to_all | solution.py:37
  23.9 0.1 all_to_all.18
  24.0 5.6 %all-gather = bf16[2,1440,40]{1,2,0:T(8,128)(2,1)S(1)} all-gather(bf16[1,1440,40]{1,2,0:T(8,128)(2,1)S(1)} %bitcast.41), channel_id=1, replica_groups=mesh['grp'=2,'exp'=8,'lat'=2] {'lat'}, dimensions={0}, use_global_device_ids=true | all-gather | bytes 345600 | tf_op jit(solution)/shard_map/all_gather | solution.py:38
  29.5 0.2 copy.22
  29.7 0.2 reshape.81
  29.9 3.5 %fusion.4 = f32[40,720]{1,0:T(8,128)S(1)} fusion(bf16[2880,40]{0,1:T(8,128)(2,1)S(1)} %reshape.81, bf16[1,2880,720]{1,2,0:T(8,128)(2,1)} %param.13), kind=kOutput, calls=%fused_computation.5 | convolution fusion | flops 165888000 | bytes 4492800 | tf_op jit(solution)/shard_map/dot_general | solution.py:41
  33.4 0.0 copy-start.1
  33.5 7.2 %fusion.6 = f32[2880,40]{1,0:T(8,128)} fusion(bf16[1,720,2880]{2,1,0:T(8,128)(2,1)} %param.15, bf16[2880,40]{0,1:T(8,128)(2,1)S(1)} %reshape.81, bf16[1,2880,720]{1,2,0:T(8,128)(2,1)} %param.14, f32[40,720]{1,0:T(8,128)S(1)} %fusion.4), kind=kOutput, calls=%fused_computation.7 | convolution fusion | flops 332006400 | bytes 9100800
  40.7 0.0 reduce-scatter.10.cloned.1.call-update
  40.7 0.0 reduce-scatter.6.cloned.1.call-start
  40.8 0.0 copy-done.1
  40.8 14.1 %all_gather.10 = bf16[64,1440]{1,0:T(8,128)(2,1)S(1)} all-gather(bf16[8,1440]{1,0:T(8,128)(2,1)S(1)} %copy-done.1), channel_id=1, replica_groups=mesh['grp'=2,'exp'=8,'lat'=2] {'exp'}, dimensions={0}, use_global_device_ids=true | all-gather | bytes 207360 | tf_op jit(solution)/shard_map/all_gather | solution.py:45
  54.8 0.0 copy-start.3
  54.8 7.6 %fusion.33 = f32[64,4096]{1,0:T(8,128)} fusion(bf16[64,1440]{1,0:T(8,128)(2,1)S(1)} %all_gather.10, bf16[1440,4096]{1,0:T(8,128)(2,1)} %param.16), kind=kOutput, calls=%fused_computation.39 | convolution fusion | flops 754974720 | bytes 13029376 | tf_op jit(solution)/shard_map/dot_general | solution.py:48
  62.4 0.0 reduce-scatter.6.cloned.1.call-update
  62.5 0.1 mul.59
  62.6 2.6 %reduce-scatter.10.cloned.1.call-done = f32[1440,40]{1,0:T(8,128)} async-done(((f32[2880,40]{1,0:T(8,128)}), f32[1440,40]{1,0:T(8,128)}) %reduce-scatter.10.cloned.1.call-update) | async-done | bytes 230416
  65.2 1.4 copy.25
  66.5 0.8 all_to_all.19
  67.3 4.6 %all-to-all-start.1 = ((f32[8,5,1440]{2,1,0:T(8,128)}), f32[8,5,1440]{2,1,0:T(8,128)S(1)}, u32[]{:S(2)}, u32[]{:S(2)}) async-start(f32[8,5,1440]{2,1,0:T(8,128)} %all_to_all.19), calls=%async_computation.1 | async-start | bytes 786432 | tf_op jit(solution)/shard_map/all_to_all | solution.py:55
  71.9 0.0 reduce-scatter.8.cloned.1.call-start
  72.0 15.8 %reduce-scatter.6.cloned.1.call-done = f32[32,4096]{1,0:T(8,128)} async-done(((f32[64,4096]{1,0:T(8,128)}), f32[32,4096]{1,0:T(8,128)}) %reduce-scatter.6.cloned.1.call-update) | async-done | bytes 524304 | tf_op jit(solution)/shard_map/reduce_scatter | solution.py:47
  87.8 0.0 copy-done.3
  87.8 1.1 maximum_convert_fusion
  88.9 0.0 copy-start
  88.9 8.7 %all_gather.11 = bf16[64,4096]{1,0:T(8,128)(2,1)S(1)} all-gather(bf16[32,4096]{1,0:T(8,128)(2,1)S(1)} %maximum_convert_fusion), channel_id=1, replica_groups=mesh['grp'=2,'exp'=8,'lat'=2] {'lat'}, dimensions={0}, use_global_device_ids=true | all-gather | bytes 786432 | tf_op jit(solution)/shard_map/all_gather | solution.py:59
  97.6 0.0 copy-start.5
  97.6 0.0 copy-start.4
  97.6 8.7 %convolution_convert_fusion = bf16[64,1440]{1,0:T(8,128)(2,1)} fusion(bf16[64,4096]{1,0:T(8,128)(2,1)S(1)} %all_gather.11, bf16[4096,1440]{0,1:T(8,128)(2,1)} %param.18), kind=kOutput, calls=%fused_computation.8 | convolution fusion | flops 755066880 | bytes 12505088 | tf_op jit(solution)/shard_map/dot_general | solution.py:58
  106.3 0.0 copy-done
  106.3 0.0 reduce-scatter.8.cloned.1.call-update
  106.3 0.1 reduce_sum.23
  106.4 0.0 copy-done.5
  106.4 0.1 copy.23
  106.5 0.0 all-to-all-done.1
  106.6 0.6 gather_fusion
  107.2 0.1 gather.7
  107.3 0.2 multiply_reduce_fusion
  107.5 0.0 copy-start.2
  107.5 29.3 %reduce-scatter.8.cloned.1.call-done = bf16[8,1440]{1,0:T(8,128)(2,1)} async-done(((bf16[64,1440]{1,0:T(8,128)(2,1)}), bf16[8,1440]{1,0:T(8,128)(2,1)}) %reduce-scatter.8.cloned.1.call-update) | async-done | bytes 23056 | tf_op jit(solution)/shard_map/reduce_scatter | solution.py:62
  136.8 0.0 copy-done.4
  136.8 1.4 add_subtract_fusion
  138.1 0.0 copy-done.2
  (7 shorter events, 0.1 us)
Async XLA Ops:
  7.2 58.0 %reduce-scatter.10.cloned.1.call-start = ((), (), s32[]{:S(2)}) async-start(), calls=%async_computation.7 | async-start | bytes 2211840
  33.4 7.3 %copy-start.1 = (bf16[8,1440]{1,0:T(8,128)(2,1)S(1)}, bf16[8,1440]{1,0:T(8,128)(2,1)}, u32[]{:S(2)}) copy-start(bf16[8,1440]{1,0:T(8,128)(2,1)} %param.10) | copy-start | bytes 69124
  40.7 47.1 %reduce-scatter.6.cloned.1.call-start = ((), (), s32[]{:S(2)}) async-start(), calls=%async_computation.5 | async-start | bytes 1572864 | tf_op jit(solution)/shard_map/reduce_scatter | solution.py:47
  54.8 32.9 %copy-start.3 = (f32[4096]{0:T(1024)S(1)}, f32[4096]{0:T(1024)}, u32[]{:S(2)}) copy-start(f32[4096]{0:T(1024)} %param.17) | copy-start | bytes 49156
  67.3 39.2 %all-to-all-start.1 = ((f32[8,5,1440]{2,1,0:T(8,128)}), f32[8,5,1440]{2,1,0:T(8,128)S(1)}, u32[]{:S(2)}, u32[]{:S(2)}) async-start(f32[8,5,1440]{2,1,0:T(8,128)} %all_to_all.19), calls=%async_computation.1 | async-start | bytes 786432 | tf_op jit(solution)/shard_map/all_to_all | solution.py:55
  71.9 64.8 %reduce-scatter.8.cloned.1.call-start = ((), (), s32[]{:S(2)}) async-start(), calls=%async_computation.6 | async-start | bytes 221184 | tf_op jit(solution)/shard_map/reduce_scatter | solution.py:62
  88.9 17.4 %copy-start = (bf16[32,4096]{1,0:T(8,128)(2,1)}, bf16[32,4096]{1,0:T(8,128)(2,1)S(1)}, u32[]{:S(2)}) copy-start(bf16[32,4096]{1,0:T(8,128)(2,1)S(1)} %maximum_convert_fusion) | copy-start | bytes 786436
  97.6 8.8 %copy-start.5 = (f32[8,4]{0,1:T(4,128)S(1)}, f32[8,4]{0,1:T(4,128)}, u32[]{:S(2)}) copy-start(f32[8,4]{0,1:T(4,128)} %param.12) | copy-start | bytes 388
  97.6 39.2 %copy-start.4 = (f32[1440]{0:T(1024)S(1)}, f32[1440]{0:T(1024)}, u32[]{:S(2)}) copy-start(f32[1440]{0:T(1024)} %param.19) | copy-start | bytes 17284
  107.5 30.6 %copy-start.2 = (bf16[8,1440]{1,0:T(8,128)(2,1)}, bf16[8,1440]{1,0:T(8,128)(2,1)S(1)}, u32[]{:S(2)}) copy-start(bf16[8,1440]{1,0:T(8,128)(2,1)S(1)} %multiply_reduce_fusion) | copy-start | bytes 69124
Sparse Core Ops, SparseCore 0:
  40.8 24.2 reduce-scatter.9
  67.4 20.3 reduce-scatter.5
  106.4 30.2 reduce-scatter.7
where the time goes:
time: 145 us
  waiting for transfers between devices  47.7 us (33%)
  blocking collectives  42.8 us (30%)
  matrix products  27.1 us (19%)
  between operations  13.9 us (10%)
  local copies, waits for them, and re-layouts  5.34 us (4%)
  starting transfers between devices  4.74 us (3%)
  other arithmetic  3.03 us (2%)
    reduce_scatter x1, waiting for transfers between devices, per_device(): lax.psum_scatter(partial_recon.astype(jnp.bfloat16), 'exp', scatter_dimen...  29.3 us
    reduce_scatter x1, waiting for transfers between devices, per_device(): lax.psum_scatter(jnp.dot(block_in, w_enc, preferred_element_type=jnp.floa...  15.8 us
    all_to_all x1, blocking collectives, per_device(): lax.all_to_all(outgoing, 'exp', split_axis=0, concat_axis=0, tiled=True)  14.5 us
    all_gather x1, blocking collectives, per_device(): gathered = lax.all_gather(tokens, 'exp', axis=0, tiled=True)  14.1 us
    all_gather x1, blocking collectives, per_device(): lax.all_gather(codes, 'lat', axis=0, tiled=True)  8.72 us
    dot_general x1, matrix products, per_device(): jnp.dot(lax.all_gather(codes, 'lat', axis=0, tiled=True), w_dec, preferre...  8.68 us
    dot_general x1, matrix products, per_device(): jnp.dot(block_in, w_enc, preferred_element_type=jnp.float32)  7.58 us
    unnamed x1, matrix products  7.23 us
  transfers between devices with their start and end apart: 4, of which 3 were waited for; matrix products, arithmetic and copies ran while one was open for 14% of the time, Pallas kernels for 0%

commit v1 on v0

v1 whole, which is shorter than its diff:
```python
import functools

import jax
import jax.numpy as jnp
from jax import lax
from jax.experimental import pallas as pl
from jax.experimental.pallas import tpu as pltpu
from jax.sharding import PartitionSpec as P

MESH = pl.DeviceIdType.MESH
F32 = jnp.float32
BF16 = jnp.bfloat16
CHUNKS = 4


def dot_nt(a, b):
    return lax.dot_general(a, b, (((1,), (1,)), ((), ())), preferred_element_type=F32)


def kernel(
    E, NL,
    tok, routes, gates, wenc, benc, wg, wu, wd, wdec, bdec,
    moe_ref, codes_ref, err_ref,
    wenc_v, wg_v, wu_v, wd_v, wdec_v,
    xall, xs, psc, own, psend, precv, call,
    phs, msend, mrecv, ms, mbs, mbr, racc, ras, rar, rbs, rbr,
    wsem, gs, gr, fs, fr, ps, pr, cs, cr, hs, hr, bs, br, as_, ar, zs, zr,
):
    R, Dl = tok.shape
    NC = CHUNKS
    Lc = codes_ref.shape[1]
    CW = Lc // NC
    T = E * R
    Tl = T // NL
    N1 = ras.shape[2]
    me = lax.axis_index("exp")
    l = lax.axis_index("lat")

    def peer(d):
        return lax.rem(me + d, E)

    def src(d):
        return lax.rem(me - d + E, E)

    def lpeer(d):
        return lax.rem(l + d, NL)

    def lsrc(d):
        return lax.rem(l - d + NL, NL)

    bar = pltpu.get_barrier_semaphore()
    for d in range(1, E):
        pl.semaphore_signal(bar, inc=1, device_id={"exp": peer(d)}, device_id_type=MESH)
    for d in range(1, NL):
        pl.semaphore_signal(bar, inc=1, device_id={"lat": lpeer(d)}, device_id_type=MESH)

    w_enc = [
        pltpu.make_async_copy(wenc.at[:, pl.ds(c * CW, CW)], wenc_v.at[c], wsem.at[c])
        for c in range(NC)
    ]
    w_g = pltpu.make_async_copy(wg, wg_v, wsem.at[NC])
    w_u = pltpu.make_async_copy(wu, wu_v, wsem.at[NC + 1])
    w_d = pltpu.make_async_copy(wd, wd_v, wsem.at[NC + 2])
    w_dec = [
        pltpu.make_async_copy(wdec.at[:, pl.ds(c * CW, CW)], wdec_v.at[c], wsem.at[NC + 3 + c])
        for c in range(NC)
    ]
    for w in w_enc + [w_g, w_u, w_d] + w_dec:
        w.start()

    xall[l, me] = tok[...]
    pl.semaphore_wait(bar, E - 1 + NL - 1)

    def to_exp(d, source, dest, ssem, rsem):
        return pltpu.make_async_remote_copy(
            src_ref=source, dst_ref=dest, send_sem=ssem, recv_sem=rsem,
            device_id={"exp": peer(d)}, device_id_type=MESH,
        )

    def to_lat(d, source, dest, ssem, rsem):
        return pltpu.make_async_remote_copy(
            src_ref=source, dst_ref=dest, send_sem=ssem, recv_sem=rsem,
            device_id={"lat": lpeer(d)}, device_id_type=MESH,
        )

    def g_copy(d):
        return to_exp(d, tok, xall.at[l, me], gs.at[d], gr.at[d])

    def g_in(d):
        return to_exp(d, tok, xall.at[l, src(d)], gs.at[d], gr.at[d])

    def f_copy(k, d):
        slot = src(k)
        return to_lat(d, xall.at[l, slot], xall.at[l, slot], fs.at[k, d], fr.at[k, d])

    def f_in(k, d):
        slot = src(k)
        return to_lat(d, xall.at[lsrc(d), slot], xall.at[lsrc(d), slot], fs.at[k, d], fr.at[k, d])

    for d in range(1, E):
        g_copy(d).start()
    for d in range(1, NL):
        f_copy(0, d).start()
    for k in range(1, E):
        g_in(k).wait_recv()
        for d in range(1, NL):
            f_copy(k, d).start()

    def rows_of(q):
        for i in range(E):
            xs[i * R:(i + 1) * R, :] = xall[q, i].astype(F32)
        return xs[...]

    def p_copy(c, d):
        return to_lat(d, psend.at[c, d], precv.at[c, d], ps.at[c, d], pr.at[c, d])

    x_own = rows_of(l).astype(BF16)
    for c in range(NC):
        w_enc[c].wait()
        part = jnp.dot(x_own, wenc_v[c], preferred_element_type=F32)
        for q in range(NL):
            psc[q] = part[q * Tl:(q + 1) * Tl, :]
        for d in range(1, NL):
            psend[c, d] = psc[lpeer(d)].astype(BF16)
            p_copy(c, d).start()
        own[c] = psc[l]

    for k in range(E):
        for d in range(1, NL):
            f_in(k, d).wait_recv()
    x_full = jnp.concatenate([rows_of(q) for q in range(NL)], axis=1).astype(BF16)
    w_g.wait()
    gate_sum = dot_nt(x_full, wg_v[...])
    w_u.wait()
    up_sum = dot_nt(x_full, wu_v[...])
    hidden = (gate_sum * jax.nn.sigmoid(1.702 * gate_sum) * (up_sum + 1.0)).astype(BF16)

    def c_copy(c, d):
        return to_lat(d, call.at[c, l], call.at[c, l], cs.at[c, d], cr.at[c, d])

    def c_in(c, d):
        return to_lat(d, call.at[c, lsrc(d)], call.at[c, lsrc(d)], cs.at[c, d], cr.at[c, d])

    for c in range(NC):
        pre = own[c]
        for d in range(1, NL):
            p_copy(c, d).wait_recv()
            pre = pre + precv[c, d].astype(F32)
        code = jnp.maximum(pre + benc[:, c * CW:(c + 1) * CW], 0.0).astype(BF16)
        call[c, l] = code
        codes_ref[:, c * CW:(c + 1) * CW] = code
        for d in range(1, NL):
            c_copy(c, d).start()

    def h_copy(d):
        return to_lat(d, msend.at[d], mrecv.at[d], hs.at[d], hr.at[d])

    w_d.wait()
    part = jnp.dot(hidden, wd_v[...], preferred_element_type=F32)
    for q in range(NL):
        phs[q] = part[:, q * Dl:(q + 1) * Dl]
    for d in range(1, NL):
        msend[d] = phs[lpeer(d)].astype(BF16)
        h_copy(d).start()

    def a_copy(d):
        return to_exp(d, ras.at[peer(d)], rar.at[d], as_.at[d], ar.at[d])

    def z_copy(d):
        return to_exp(d, rbs.at[peer(d)], rbr.at[d], zs.at[d], zr.at[d])

    def b_copy(d):
        return to_exp(d, mbs.at[peer(d)], mbr.at[d], bs.at[d], br.at[d])

    def codes_of(c):
        return call[c].reshape(T, CW)

    for c in range(NC):
        for d in range(1, NL):
            c_in(c, d).wait_recv()
        w_dec[c].wait()
        term = dot_nt(codes_of(c), wdec_v[c, 0:N1, :])
        if c == 0:
            racc[:, 0:N1] = term
        else:
            racc[:, 0:N1] += term
    for i in range(E):
        ras[i] = racc[i * R:(i + 1) * R, 0:N1].astype(BF16)
    for d in range(1, E):
        a_copy(d).start()

    total = phs[l]
    for d in range(1, NL):
        h_copy(d).wait_recv()
        total = total + mrecv[d].astype(F32)
    ms[...] = total
    for i in range(E):
        mbs[i] = ms[i * R:(i + 1) * R, :].astype(BF16)
    for d in range(1, E):
        b_copy(d).start()

    for c in range(NC):
        term = dot_nt(codes_of(c), wdec_v[c, N1:Dl, :])
        if c == 0:
            racc[:, N1:Dl] = term
        else:
            racc[:, N1:Dl] += term
    for i in range(E):
        rbs[i] = racc[i * R:(i + 1) * R, N1:Dl].astype(BF16)
    for d in range(1, E):
        z_copy(d).start()

    eye = lax.broadcasted_iota(jnp.int32, (R, R), 0) == lax.broadcasted_iota(jnp.int32, (R, R), 1)

    def weight_of(e):
        line = jnp.sum(jnp.where(routes[...] == e, gates[...], 0.0), axis=0, keepdims=True)
        return jnp.sum(jnp.where(eye, jnp.broadcast_to(line, (R, R)), 0.0), axis=1, keepdims=True)

    mine = pl.ds(pl.multiple_of(me * R, R), R)
    moe = weight_of(me) * ms[mine, :]
    for d in range(1, E):
        b_copy(d).wait_recv()
        moe = moe + weight_of(src(d)) * mbr[d].astype(F32)
    moe = moe.astype(BF16)
    moe_ref[...] = moe
    err_ref[...] = moe.astype(F32) - bdec[...]

    first = racc[mine, 0:N1]
    for d in range(1, E):
        a_copy(d).wait_recv()
        first = first + rar[d].astype(F32)
    err_ref[:, 0:N1] = err_ref[:, 0:N1] - first
    last = racc[mine, N1:Dl]
    for d in range(1, E):
        z_copy(d).wait_recv()
        last = last + rbr[d].astype(F32)
    err_ref[:, N1:Dl] = err_ref[:, N1:Dl] - last

    for d in range(1, E):
        g_copy(d).wait_send()
        a_copy(d).wait_send()
        b_copy(d).wait_send()
        z_copy(d).wait_send()
    for d in range(1, NL):
        for k in range(E):
            f_copy(k, d).wait_send()
        for c in range(NC):
            p_copy(c, d).wait_send()
            c_copy(c, d).wait_send()
        h_copy(d).wait_send()


def per_device(E, NL, tokens, routes, gates, w_gate, w_up, w_down, w_enc, b_enc, w_dec, b_dec):
    R, Dl = tokens.shape
    D = w_down.shape[2]
    F = w_down.shape[1]
    Lc = w_enc.shape[1]
    NC = CHUNKS
    CW = Lc // NC
    T = E * R
    Tl = T // NL
    N1 = pl.cdiv(pl.cdiv(Dl, 2), 128) * 128
    N2 = Dl - N1
    hbm = pl.BlockSpec(memory_space=pl.ANY)
    vmem = pl.BlockSpec(memory_space=pltpu.VMEM)
    dma = pltpu.SemaphoreType.DMA
    return pl.pallas_call(
        functools.partial(kernel, E, NL),
        out_shape=(
            jax.ShapeDtypeStruct((R, Dl), BF16),
            jax.ShapeDtypeStruct((Tl, Lc), BF16),
            jax.ShapeDtypeStruct((R, Dl), F32),
        ),
        in_specs=[vmem, vmem, vmem, hbm, vmem, hbm, hbm, hbm, hbm, vmem],
        out_specs=(vmem, vmem, vmem),
        scratch_shapes=[
            pltpu.VMEM((NC, Dl, CW), BF16),
            pltpu.VMEM((F, D), BF16),
            pltpu.VMEM((F, D), BF16),
            pltpu.VMEM((F, D), BF16),
            pltpu.VMEM((NC, Dl, CW), BF16),
            pltpu.VMEM((NL, E, R, Dl), BF16),
            pltpu.VMEM((T, Dl), F32),
            pltpu.VMEM((NL, Tl, CW), F32),
            pltpu.VMEM((NC, Tl, CW), F32),
            pltpu.VMEM((NC, NL, Tl, CW), BF16),
            pltpu.VMEM((NC, NL, Tl, CW), BF16),
            pltpu.VMEM((NC, NL, Tl, CW), BF16),
            pltpu.VMEM((NL, T, Dl), F32),
            pltpu.VMEM((NL, T, Dl), BF16),
            pltpu.VMEM((NL, T, Dl), BF16),
            pltpu.VMEM((T, Dl), F32),
            pltpu.VMEM((E, R, Dl), BF16),
            pltpu.VMEM((E, R, Dl), BF16),
            pltpu.VMEM((T, Dl), F32),
            pltpu.VMEM((E, R, N1), BF16),
            pltpu.VMEM((E, R, N1), BF16),
            pltpu.VMEM((E, R, N2), BF16),
            pltpu.VMEM((E, R, N2), BF16),
            dma((2 * NC + 3,)),
            dma((E,)), dma((E,)),
            dma((E, NL)), dma((E, NL)),
            dma((NC, NL)), dma((NC, NL)),
            dma((NC, NL)), dma((NC, NL)),
            dma((NL,)), dma((NL,)),
            dma((E,)), dma((E,)),
            dma((E,)), dma((E,)),
            dma((E,)), dma((E,)),
        ],
        compiler_params=pltpu.CompilerParams(
            collective_id=0, has_side_effects=True, vmem_limit_bytes=58 * 1024 * 1024
        ),
    )(
        tokens, routes.T, gates.T, w_enc, b_enc.reshape(1, -1),
        w_gate[0].T, w_up[0].T, w_down[0], w_dec.T, b_dec.reshape(1, -1),
    )


def solution(mesh):
    placed = (
        P(("grp", "exp"), "lat"),
        P(("grp", "exp"), None),
        P(("grp", "exp"), None),
        P("exp", None, "lat"),
        P("exp", None, "lat"),
        P("exp", "lat", None),
        P("lat", "exp"),
        P("exp"),
        P("exp", "lat"),
        P("lat"),
    )
    return jax.shard_map(
        functools.partial(per_device, mesh.shape["exp"], mesh.shape["lat"]),
        mesh=mesh,
        in_specs=placed,
        out_specs=(P(("grp", "exp"), "lat"), P(("grp", "lat"), "exp"), P(("grp", "exp"), "lat")),
        check_vma=False,
    )
```

time: 145 us -> 46.8 us (0.32)
  waiting for transfers between devices: 47.7 us -> 0 us
  blocking collectives: 42.8 us -> 0 us
  Pallas kernels: 0 us -> 40 us
  matrix products: 27.1 us -> 0 us
  between operations: 13.9 us -> 0.64 us
  starting transfers between devices: 4.74 us -> 0 us
  other arithmetic: 3.03 us -> 0 us
    reduce_scatter x2 -> x0, waiting for transfers between devices: 45 us -> none  [the longest x1 29.3 us: per_device(): lax.psum_scatter(partial_recon.astype(jnp.bfloat16), 'exp', scatter_dimen...]
    pallas_call x0 -> x1, Pallas kernels: none -> 40 us  [per_device(): pl.pallas_call(functools.partial(kernel, E, NL), out_shape=(jax.ShapeDtyp...]
    all_gather x3 -> x0, blocking collectives: 28.3 us -> none  [the longest x1 14.1 us: per_device(): gathered = lax.all_gather(tokens, 'exp', axis=0, tiled=True)]
    dot_general x4 -> x0, matrix products: 19.9 us -> none  [the longest x1 8.68 us: per_device(): jnp.dot(lax.all_gather(codes, 'lat', axis=0, tiled=True), w_dec, preferre...]
    all_to_all x1 -> x0, blocking collectives: 14.5 us -> none  [per_device(): lax.all_to_all(outgoing, 'exp', split_axis=0, concat_axis=0, tiled=True)]
    unnamed x1 -> x0, matrix products: 7.23 us -> none
    all_to_all x1 -> x0, starting transfers between devices: 4.63 us -> none  [per_device(): lax.all_to_all(shares, 'exp', split_axis=0, concat_axis=0, tiled=True)]
    unnamed x4 -> x0, waiting for transfers between devices: 2.66 us -> none
  transfers between devices with their start and end apart: 4 -> 0, of which waited for: 3 -> 0; matrix products, arithmetic and copies ran while one was open for 14% -> 0% of each run, Pallas kernels for 0% -> 0%
where the time goes in v1:
time: 46.8 us; the launch traced here: 46.4 us
  Pallas kernels  40 us (85%)
  local copies, waits for them, and re-layouts  5.73 us (12%)
  between operations  0.64 us (1%)
    pallas_call x1, Pallas kernels, per_device(): pl.pallas_call(functools.partial(kernel, E, NL), out_shape=(jax.ShapeDtyp...  40 us
    unnamed x3, local copies, waits for them, and re-layouts  4.44 us
    reshape x1, local copies, waits for them, and re-layouts, per_device(): b_dec.reshape(1, -1)  1.3 us

profile of v1, /device:TPU:0, one launch (start us, length us, event | category | flops | bytes accessed | tf_op | source)
XLA Modules:
  0.0 46.4 jit_solution(9985317415622881002)
XLA Ops:
  0.6 1.3 %reshape.13.bdec = f32[1,1440]{1,0:T(1,128)} reshape(f32[1440]{0:T(1024)} %param.19) | data formatting | bytes 11520 | tf_op jit(solution)/shard_map/reshape | solution.py:315
  1.9 40.0 %shard_map.121 = (bf16[8,1440]{1,0:T(8,128)(2,1)}, bf16[32,4096]{1,0:T(8,128)(2,1)}, f32[8,1440]{1,0:T(8,128)}) custom-call(bf16[8,1440]{1,0:T(8,128)(2,1)} %tok.1, s32[4,8]{1,0:T(4,128)} %bitcast.16, f32[4,8]{1,0:T(4,128)} %bitcast.17, bf16[1440,4096]{1,0:T(8,128)(2,1)} %wenc.1, f32[1,4096]{1,0:T(1,128)} %bitcast.15, bf16[720,2880]{1,0:T(8,128)(2,1)} %bitcast.12, ...), custom_call_target="tpu_custom_call" | custom-call | tf_op jit(solution)/shard_map/pallas_call | solution.py:267
  42.0 1.3 %copy.16 = bf16[8,1440]{1,0:T(8,128)(2,1)} copy(bf16[8,1440]{1,0:T(8,128)(2,1)} %get-tuple-element.6) | data formatting | bytes 46080
  43.3 1.7 %copy.17 = bf16[32,4096]{1,0:T(8,128)(2,1)} copy(bf16[32,4096]{1,0:T(8,128)(2,1)} %get-tuple-element.7) | data formatting | bytes 524288
  45.0 1.4 %copy.18 = f32[8,1440]{1,0:T(8,128)} copy(f32[8,1440]{1,0:T(8,128)} %get-tuple-element.8) | data formatting | bytes 92160

commit v2 on v1

--- a/solution.py
+++ b/solution.py
@@ -141,7 +141,7 @@
     def c_in(c, d):
         return to_lat(d, call.at[c, lsrc(d)], call.at[c, lsrc(d)], cs.at[c, d], cr.at[c, d])
 
-    for c in range(NC):
+    def finish_codes(c):
         pre = own[c]
         for d in range(1, NL):
             p_copy(c, d).wait_recv()
@@ -152,6 +152,9 @@
         for d in range(1, NL):
             c_copy(c, d).start()
 
+    for c in range(NC // 2):
+        finish_codes(c)
+
     def h_copy(d):
         return to_lat(d, msend.at[d], mrecv.at[d], hs.at[d], hr.at[d])
 
@@ -162,6 +165,8 @@
     for d in range(1, NL):
         msend[d] = phs[lpeer(d)].astype(BF16)
         h_copy(d).start()
+    for c in range(NC // 2, NC):
+        finish_codes(c)
 
     def a_copy(d):
         return to_exp(d, ras.at[peer(d)], rar.at[d], as_.at[d], ar.at[d])
@@ -175,19 +180,22 @@
     def codes_of(c):
         return call[c].reshape(T, CW)
 
-    for c in range(NC):
+    def add(c, low, high):
+        term = dot_nt(codes_of(c), wdec_v[c, low:high, :])
+        if c == 0:
+            racc[:, low:high] = term
+        else:
+            racc[:, low:high] += term
+
+    def arrive(c):
         for d in range(1, NL):
             c_in(c, d).wait_recv()
         w_dec[c].wait()
-        term = dot_nt(codes_of(c), wdec_v[c, 0:N1, :])
-        if c == 0:
-            racc[:, 0:N1] = term
-        else:
-            racc[:, 0:N1] += term
-    for i in range(E):
-        ras[i] = racc[i * R:(i + 1) * R, 0:N1].astype(BF16)
-    for d in range(1, E):
-        a_copy(d).start()
+
+    for c in range(NC // 2):
+        arrive(c)
+        add(c, 0, N1)
+        add(c, N1, Dl)
 
     total = phs[l]
     for d in range(1, NL):
@@ -199,12 +207,15 @@
     for d in range(1, E):
         b_copy(d).start()
 
-    for c in range(NC):
-        term = dot_nt(codes_of(c), wdec_v[c, N1:Dl, :])
-        if c == 0:
-            racc[:, N1:Dl] = term
-        else:
-            racc[:, N1:Dl] += term
+    for c in range(NC // 2, NC):
+        arrive(c)
+        add(c, 0, N1)
+        if c == NC - 1:
+            for i in range(E):
+                ras[i] = racc[i * R:(i + 1) * R, 0:N1].astype(BF16)
+            for d in range(1, E):
+                a_copy(d).start()
+        add(c, N1, Dl)
     for i in range(E):
         rbs[i] = racc[i * R:(i + 1) * R, N1:Dl].astype(BF16)
     for d in range(1, E):
@@ -223,7 +234,7 @@
         moe = moe + weight_of(src(d)) * mbr[d].astype(F32)
     moe = moe.astype(BF16)
     moe_ref[...] = moe
-    err_ref[...] = moe.astype(F32) - bdec[...]
+    err_ref[...] = moe.astype(F32) - bdec[...].reshape(1, Dl)
 
     first = racc[mine, 0:N1]
     for d in range(1, E):
@@ -248,6 +259,12 @@
             p_copy(c, d).wait_send()
             c_copy(c, d).wait_send()
         h_copy(d).wait_send()
+
+
+def hand_over(a, b, c, a_out, b_out, c_out):
+    a_out[...] = a[...]
+    b_out[...] = b[...]
+    c_out[...] = c[...]
 
 
 def per_device(E, NL, tokens, routes, gates, w_gate, w_up, w_down, w_enc, b_enc, w_dec, b_dec):
@@ -264,7 +281,7 @@
     hbm = pl.BlockSpec(memory_space=pl.ANY)
     vmem = pl.BlockSpec(memory_space=pltpu.VMEM)
     dma = pltpu.SemaphoreType.DMA
-    return pl.pallas_call(
+    results = pl.pallas_call(
         functools.partial(kernel, E, NL),
         out_shape=(
             jax.ShapeDtypeStruct((R, Dl), BF16),
@@ -312,8 +329,14 @@
         ),
     )(
         tokens, routes.T, gates.T, w_enc, b_enc.reshape(1, -1),
-        w_gate[0].T, w_up[0].T, w_down[0], w_dec.T, b_dec.reshape(1, -1),
+        w_gate[0].T, w_up[0].T, w_down[0], w_dec.T, b_dec,
     )
+    return pl.pallas_call(
+        hand_over,
+        out_shape=tuple(jax.ShapeDtypeStruct(r.shape, r.dtype) for r in results),
+        in_specs=[vmem] * 3,
+        out_specs=(vmem,) * 3,
+    )(*results)
 
 
 def solution(mesh):

time: 46.8 us -> 42.5 us (0.908)
  local copies, waits for them, and re-layouts: 5.73 us -> 0 us
  Pallas kernels: 40 us -> 41.7 us
    unnamed x3 -> x0, local copies, waits for them, and re-layouts: 4.44 us -> none
    pallas_call x0 -> x1, Pallas kernels: none -> 1.68 us  [per_device(): pl.pallas_call(hand_over, out_shape=tuple((jax.ShapeDtypeStruct(r.shape,...]
    reshape x1 -> x0, local copies, waits for them, and re-layouts: 1.3 us -> none  [per_device(): b_dec.reshape(1, -1)]
where the time goes in v2:
time: 42.5 us; the launch traced here: 42.3 us
  Pallas kernels  41.7 us (98%)
  between operations  0.64 us (2%)
    pallas_call x1, Pallas kernels, per_device(): pl.pallas_call(functools.partial(kernel, E, NL), out_shape=(jax.ShapeDtyp...  40 us
    pallas_call x1, Pallas kernels, per_device(): pl.pallas_call(hand_over, out_shape=tuple((jax.ShapeDtypeStruct(r.shape,...  1.68 us

profile of v2, /device:TPU:0, one launch (start us, length us, event | category | flops | bytes accessed | tf_op | source)
XLA Modules:
  0.0 42.3 jit_solution(7829876163776238020)
XLA Ops:
  0.6 40.0 %shard_map.121 = (bf16[8,1440]{1,0:T(8,128)(2,1)}, bf16[32,4096]{1,0:T(8,128)(2,1)}, f32[8,1440]{1,0:T(8,128)}) custom-call(bf16[8,1440]{1,0:T(8,128)(2,1)} %tok.1, s32[4,8]{1,0:T(4,128)} %bitcast.16, f32[4,8]{1,0:T(4,128)} %bitcast.17, bf16[1440,4096]{1,0:T(8,128)(2,1)} %wenc.1, f32[1,4096]{1,0:T(1,128)} %bitcast.15, bf16[720,2880]{1,0:T(8,128)(2,1)} %bitcast.12, ...), custom_call_target="tpu_custom_call" | custom-call | tf_op jit(solution)/shard_map/pallas_call | solution.py:284
  40.6 1.7 %shard_map.122 = (bf16[8,1440]{1,0:T(8,128)(2,1)}, bf16[32,4096]{1,0:T(8,128)(2,1)}, f32[8,1440]{1,0:T(8,128)}) custom-call(bf16[8,1440]{1,0:T(8,128)(2,1)} %get-tuple-element.6.a, bf16[32,4096]{1,0:T(8,128)(2,1)} %get-tuple-element.7.b, f32[8,1440]{1,0:T(8,128)} %get-tuple-element.8.c), custom_call_target="tpu_custom_call" | custom-call | tf_op jit(solution)/shard_map/pallas_call | solution.py:334
